TPU v7x, 32 devices: a whole 2x2x4 slice. The times are simulated.
32 devices in a mesh: node: 8 (over y, x, core), local: 4 (over z).
Axes of the slice: x: 2, y: 2, z: 4, core: 2. Of those that a mesh axis runs over, the one named last changes fastest.
Arguments:
- grad_out: bfloat16 [4096, 32, 384], P(('node', 'local')), may hold values from -6 to 6
- pooled: bfloat16 [4096, 32, 256], P(('node', 'local')), may hold values from -6 to 6
- proj: bfloat16 [32, 256, 128], P(('node', 'local')), may hold values from -0.5 to 0.5
- assign: int32 [32], replicated, may hold values from 0 to 31, each once
- indices: int32 [32, 4096, 3, 8], P(('node', 'local')), may hold values from 0 to 511
- lengths: int32 [32, 4096, 3], P(('node', 'local')), may hold values from 1 to 8
Outputs:
- table_grad: float32 [32, 512, 256], P(('node', 'local'))
- proj_grad: float32 [32, 256, 128], P(('node', 'local'))
Inputs may be any that keep to these rules, and one draw needn't show every extreme that they name: assign holds every group id once.
All inputs are finite; a program needn't handle non-finite values.
Results may differ from a plain program's by a relative error of at most 0.0029.
Values may be sent and summed in bfloat16 or wider, within the bound.
No kernel may reach another device: no remote copies, remote signals or barrier semaphores. Data moves between devices by JAX's collectives and lax.ppermute only.
A program may use at most 192 MiB of HBM per device.

v0:
```python
import math

import jax
import jax.numpy as jnp
from jax import lax
from jax.sharding import PartitionSpec as P

ROWS = 512
W1 = 16
W2 = 48
W3 = 192
PD = 128


def deliver(sending):
    count, slots, width = sending.shape
    moved = lax.all_to_all(sending, ("node", "local"), split_axis=1, concat_axis=0, tiled=True)
    return moved.reshape(-1, width)


def local(grad_out, pooled, proj, assign, indices, lengths):
    widths = (W1, W2, W3)
    count = grad_out.shape[0]
    slots = assign.shape[0]
    scale = 1.0 / math.sqrt(count * slots)
    grad_send = jnp.take(grad_out, assign, axis=1)
    pool_send = jnp.take(pooled, assign, axis=1)
    grad_recv = deliver(grad_send)
    pieces = []
    offset = 0
    for partial_table, partial_width in enumerate(widths):
        pieces.append(
            jnp.einsum(
                "bsw,bso->swo",
                pool_send[:, :, offset : offset + partial_width],
                grad_send[:, :, partial_table * PD : (partial_table + 1) * PD],
                preferred_element_type=jnp.float32,
            )
        )
        offset = offset + partial_width
    proj_grad = lax.psum_scatter(
        jnp.concatenate(pieces, axis=1) * scale, ("node", "local"), scatter_dimension=0, tiled=True
    )
    weights = proj[0]
    lookups = indices[0]
    counts = lengths[0]
    total_rows = grad_recv.shape[0]
    lookup_count = lookups.shape[2]
    dpool_parts = []
    offset = 0
    for table, width in enumerate(widths):
        grad_part = grad_recv[:, table * PD : (table + 1) * PD]
        dpool_parts.append(
            lax.dot_general(
                grad_part,
                weights[offset : offset + width],
                (((1,), (1,)), ((), ())),
                preferred_element_type=jnp.float32,
            ).astype(jnp.bfloat16)
        )
        offset = offset + width
    dpool_all = jnp.concatenate(dpool_parts, axis=1)
    block = min(1024, total_rows)
    blocks = total_rows // block
    dpool_blocks = dpool_all.reshape(blocks, block, dpool_all.shape[1])
    lookup_blocks = lookups.reshape(blocks, block, 3, lookup_count)
    count_blocks = counts.reshape(blocks, block, 3)
    row_ids = jnp.arange(ROWS, dtype=jnp.int32)

    def accumulate(carry, items):
        dpool_block, lookup_block, count_block = items
        pieces = []
        offset = 0
        for table, width in enumerate(widths):
            hits = jnp.zeros((block, ROWS), jnp.bfloat16)
            for lookup in range(lookup_count):
                match = (lookup_block[:, table, lookup][:, None] == row_ids[None, :]) & (
                    count_block[:, table] > lookup
                )[:, None]
                hits = hits + match.astype(jnp.bfloat16)
            pieces.append(
                lax.dot_general(
                    hits,
                    dpool_block[:, offset : offset + width],
                    (((0,), (0,)), ((), ())),
                    preferred_element_type=jnp.float32,
                )
            )
            offset = offset + width
        return (carry + jnp.concatenate(pieces, axis=1), None)

    start_total = jnp.zeros((ROWS, dpool_all.shape[1]), jnp.float32)
    table_total, unused = lax.scan(
        accumulate, start_total, (dpool_blocks, lookup_blocks, count_blocks)
    )
    table_grad = table_total[None]
    return (table_grad, proj_grad)


def solution(mesh):
    placed = (
        P(("node", "local"), None, None),
        P(("node", "local"), None, None),
        P(("node", "local"), None, None),
        P(),
        P(("node", "local"), None, None, None),
        P(("node", "local"), None, None),
    )
    return jax.shard_map(
        local,
        mesh=mesh,
        in_specs=placed,
        out_specs=(P(("node", "local"), None, None), P(("node", "local"), None, None)),
        check_vma=False,
    )
```

profile of v0, /device:TPU:13, one launch (start us, length us, event | category | flops | bytes accessed | tf_op | source)
XLA Modules:
  0.0 241.3 jit_solution(12654475472859068248)
XLA Ops:
  9.1 11.2 %gather_fusion = bf16[32,128,384]{2,0,1:T(8,128)(2,1)} fusion(bf16[128,32,384]{2,1,0:T(8,128)(2,1)S(1)} %copy-done, s32[1024]{0:T(1024)S(1)} %pad_clamp_fusion), kind=kCustom, calls=%fused_computation | custom fusion | bytes 6291584 | tf_op jit(solution)/shard_map/jit(_take)/gather | solution.py:26
  20.3 4.7 %fusion.134 = bf16[128,32,384]{2,0,1:T(8,128)(2,1)} fusion(bf16[32,128,384]{2,0,1:T(8,128)(2,1)} %gather_fusion, pred[32]{0:T(512)(128)(4,1)S(1)} %compare_and_fusion), kind=kLoop, calls=%fused_computation.177 | loop fusion | flops 1572864 | bytes 6291488 | tf_op jit(solution)/shard_map/jit(_take)/select_n | solution.py:26
  25.0 6.4 %all-to-all-start = ((bf16[128,32,384]{2,0,1:T(8,128)(2,1)}), bf16[128,32,384]{2,0,1:T(8,128)(2,1)}, u32[]{:S(2)}, u32[]{:S(2)}) async-start(bf16[128,32,384]{2,0,1:T(8,128)(2,1)} %fusion.134), calls=%async_computation | async-start | bytes 6291456 | tf_op jit(solution)/shard_map/all_to_all | solution.py:17
  31.6 7.5 %gather_fusion.1 = bf16[32,128,256]{2,0,1:T(8,128)(2,1)} fusion(bf16[128,32,256]{2,1,0:T(8,128)(2,1)} %param.9, s32[1024]{0:T(1024)S(1)} %pad_clamp_fusion), kind=kCustom, calls=%fused_computation.1 | custom fusion | bytes 4194432 | tf_op jit(solution)/shard_map/jit(_take)/gather | solution.py:27
  39.1 4.5 %copy.20 = bf16[32,128,256]{1,2,0:T(8,128)(2,1)} copy(bf16[32,128,256]{2,0,1:T(8,128)(2,1)} %gather_fusion.1) | data formatting | bytes 4194304 | tf_op jit(solution)/shard_map/jit(_take)/gather | solution.py:27
  47.5 2.3 maximum_multiply_fusion
  53.4 97.8 %all-to-all-done = bf16[128,32,384]{2,0,1:T(8,128)(2,1)} async-done(((bf16[128,32,384]{2,0,1:T(8,128)(2,1)}), bf16[128,32,384]{2,0,1:T(8,128)(2,1)}, u32[]{:S(2)}, u32[]{:S(2)}) %all-to-all-start) | async-done | bytes 3145760 | tf_op jit(solution)/shard_map/all_to_all | solution.py:17
  157.8 4.1 %copy.21 = bf16[4096,256]{1,0:T(8,128)(2,1)} copy(bf16[4096,256]{0,1:T(8,128)(2,1)} %pad_maximum_fusion) | data formatting | bytes 4194304
  161.9 70.5 %while.12 = (s32[]{:T(128)}, f32[512,256]{0,1:T(8,128)}, s32[4,1024,3,8]{1,0,3,2:T(4,128)}, s32[4,1024,3]{1,0,2:T(4,128)}, bf16[4,1024,256]{2,1,0:T(8,128)(2,1)}, /*index=5*/s32[]{:T(128)}, s32[]{:T(128)}) while((s32[]{:T(128)}, f32[512,256]{0,1:T(8,128)}, s32[4,1024,3,8]{1,0,3,2:T(4,128)}, s32[4,1024,3]{1,0,2:T(4,128)}, ...), condition=%wide.region_1.2_spmd.clone.clone, body=%wide.region_0.1_spmd.clone.clone.sunk | while | flops 331898880 | bytes 4993131 | solution.py:93
  165.3 3.8 %fusion.173 = f32[512,192]{0,1:T(8,128)S(1)} fusion(s32[1024]{0:T(1024)S(1)} %bitcast.129, s32[1024]{0:T(1024)S(1)} %bitcast.130, s32[1024]{0:T(1024)S(1)} %bitcast.131, s32[1024]{0:T(1024)S(1)} %bitcast.132, s32[1024]{0:T(1024)S(1)} %bitcast.133, s32[1024]{0:T(1024)S(1)} %bitcast.134, s32[1024]{0:T(1024)S(1)} %bitcast.135, s32[1024]{0:T(1024)S(1)} %bitcast.136, ...), kind=kOutput, calls=%fused_computation.76.clone.1 | convolution fusion | flops 222298112 | bytes 958464 | tf_op jit(solution)/shard_map/while/body/eval_jaxpr/dot_general | solution.py:82
  169.1 4.4 %fusion.174 = f32[512,48]{0,1:T(8,128)} fusion(s32[1024]{0:T(1024)S(1)} %bitcast.121, s32[1024]{0:T(1024)S(1)} %bitcast.122, s32[1024]{0:T(1024)S(1)} %bitcast.123, s32[1024]{0:T(1024)S(1)} %bitcast.124, s32[1024]{0:T(1024)S(1)} %bitcast.125, s32[1024]{0:T(1024)S(1)} %bitcast.126, s32[1024]{0:T(1024)S(1)} %bitcast.127, s32[1024]{0:T(1024)S(1)} %bitcast.128, ...), kind=kOutput, calls=%fused_computation.84.clone.1 | convolution fusion | flops 71303168 | bytes 401408 | tf_op jit(solution)/shard_map/while/body/eval_jaxpr/dot_general | solution.py:82
  173.5 4.0 %fusion.176 = f32[512,16]{0,1:T(8,128)} fusion(s32[1024]{0:T(1024)S(1)} %bitcast.119, s32[1024]{0:T(1024)S(1)} %bitcast.120, s32[1024]{0:T(1024)S(1)} %bitcast.138, s32[1024]{0:T(1024)S(1)} %bitcast.139, s32[1024]{0:T(1024)S(1)} %bitcast.140, s32[1024]{0:T(1024)S(1)} %bitcast.141, s32[1024]{0:T(1024)S(1)} %bitcast.137, s32[1024]{0:T(1024)S(1)} %bitcast.118, ...), kind=kOutput, calls=%fused_computation.114.clone.1 | convolution fusion | flops 37748736 | bytes 335872 | tf_op jit(solution)/shard_map/while/body/eval_jaxpr/dot_general | solution.py:82
  182.8 3.8 %fusion.173 = f32[512,192]{0,1:T(8,128)S(1)} fusion(s32[1024]{0:T(1024)S(1)} %bitcast.129, s32[1024]{0:T(1024)S(1)} %bitcast.130, s32[1024]{0:T(1024)S(1)} %bitcast.131, s32[1024]{0:T(1024)S(1)} %bitcast.132, s32[1024]{0:T(1024)S(1)} %bitcast.133, s32[1024]{0:T(1024)S(1)} %bitcast.134, s32[1024]{0:T(1024)S(1)} %bitcast.135, s32[1024]{0:T(1024)S(1)} %bitcast.136, ...), kind=kOutput, calls=%fused_computation.76.clone.1 | convolution fusion | flops 222298112 | bytes 958464 | tf_op jit(solution)/shard_map/while/body/eval_jaxpr/dot_general | solution.py:82
  186.5 4.4 %fusion.174 = f32[512,48]{0,1:T(8,128)} fusion(s32[1024]{0:T(1024)S(1)} %bitcast.121, s32[1024]{0:T(1024)S(1)} %bitcast.122, s32[1024]{0:T(1024)S(1)} %bitcast.123, s32[1024]{0:T(1024)S(1)} %bitcast.124, s32[1024]{0:T(1024)S(1)} %bitcast.125, s32[1024]{0:T(1024)S(1)} %bitcast.126, s32[1024]{0:T(1024)S(1)} %bitcast.127, s32[1024]{0:T(1024)S(1)} %bitcast.128, ...), kind=kOutput, calls=%fused_computation.84.clone.1 | convolution fusion | flops 71303168 | bytes 401408 | tf_op jit(solution)/shard_map/while/body/eval_jaxpr/dot_general | solution.py:82
  191.0 4.0 %fusion.176 = f32[512,16]{0,1:T(8,128)} fusion(s32[1024]{0:T(1024)S(1)} %bitcast.119, s32[1024]{0:T(1024)S(1)} %bitcast.120, s32[1024]{0:T(1024)S(1)} %bitcast.138, s32[1024]{0:T(1024)S(1)} %bitcast.139, s32[1024]{0:T(1024)S(1)} %bitcast.140, s32[1024]{0:T(1024)S(1)} %bitcast.141, s32[1024]{0:T(1024)S(1)} %bitcast.137, s32[1024]{0:T(1024)S(1)} %bitcast.118, ...), kind=kOutput, calls=%fused_computation.114.clone.1 | convolution fusion | flops 37748736 | bytes 335872 | tf_op jit(solution)/shard_map/while/body/eval_jaxpr/dot_general | solution.py:82
  195.0 2.0 maximum_add_fusion.2
  200.5 3.7 %fusion.173 = f32[512,192]{0,1:T(8,128)S(1)} fusion(s32[1024]{0:T(1024)S(1)} %bitcast.129, s32[1024]{0:T(1024)S(1)} %bitcast.130, s32[1024]{0:T(1024)S(1)} %bitcast.131, s32[1024]{0:T(1024)S(1)} %bitcast.132, s32[1024]{0:T(1024)S(1)} %bitcast.133, s32[1024]{0:T(1024)S(1)} %bitcast.134, s32[1024]{0:T(1024)S(1)} %bitcast.135, s32[1024]{0:T(1024)S(1)} %bitcast.136, ...), kind=kOutput, calls=%fused_computation.76.clone.1 | convolution fusion | flops 222298112 | bytes 958464 | tf_op jit(solution)/shard_map/while/body/eval_jaxpr/dot_general | solution.py:82
  204.2 4.4 %fusion.174 = f32[512,48]{0,1:T(8,128)} fusion(s32[1024]{0:T(1024)S(1)} %bitcast.121, s32[1024]{0:T(1024)S(1)} %bitcast.122, s32[1024]{0:T(1024)S(1)} %bitcast.123, s32[1024]{0:T(1024)S(1)} %bitcast.124, s32[1024]{0:T(1024)S(1)} %bitcast.125, s32[1024]{0:T(1024)S(1)} %bitcast.126, s32[1024]{0:T(1024)S(1)} %bitcast.127, s32[1024]{0:T(1024)S(1)} %bitcast.128, ...), kind=kOutput, calls=%fused_computation.84.clone.1 | convolution fusion | flops 71303168 | bytes 401408 | tf_op jit(solution)/shard_map/while/body/eval_jaxpr/dot_general | solution.py:82
  208.6 4.0 %fusion.176 = f32[512,16]{0,1:T(8,128)} fusion(s32[1024]{0:T(1024)S(1)} %bitcast.119, s32[1024]{0:T(1024)S(1)} %bitcast.120, s32[1024]{0:T(1024)S(1)} %bitcast.138, s32[1024]{0:T(1024)S(1)} %bitcast.139, s32[1024]{0:T(1024)S(1)} %bitcast.140, s32[1024]{0:T(1024)S(1)} %bitcast.141, s32[1024]{0:T(1024)S(1)} %bitcast.137, s32[1024]{0:T(1024)S(1)} %bitcast.118, ...), kind=kOutput, calls=%fused_computation.114.clone.1 | convolution fusion | flops 37748736 | bytes 335872 | tf_op jit(solution)/shard_map/while/body/eval_jaxpr/dot_general | solution.py:82
  212.7 2.0 maximum_add_fusion.2
  218.1 3.7 %fusion.173 = f32[512,192]{0,1:T(8,128)S(1)} fusion(s32[1024]{0:T(1024)S(1)} %bitcast.129, s32[1024]{0:T(1024)S(1)} %bitcast.130, s32[1024]{0:T(1024)S(1)} %bitcast.131, s32[1024]{0:T(1024)S(1)} %bitcast.132, s32[1024]{0:T(1024)S(1)} %bitcast.133, s32[1024]{0:T(1024)S(1)} %bitcast.134, s32[1024]{0:T(1024)S(1)} %bitcast.135, s32[1024]{0:T(1024)S(1)} %bitcast.136, ...), kind=kOutput, calls=%fused_computation.76.clone.1 | convolution fusion | flops 222298112 | bytes 958464 | tf_op jit(solution)/shard_map/while/body/eval_jaxpr/dot_general | solution.py:82
  221.9 4.4 %fusion.174 = f32[512,48]{0,1:T(8,128)} fusion(s32[1024]{0:T(1024)S(1)} %bitcast.121, s32[1024]{0:T(1024)S(1)} %bitcast.122, s32[1024]{0:T(1024)S(1)} %bitcast.123, s32[1024]{0:T(1024)S(1)} %bitcast.124, s32[1024]{0:T(1024)S(1)} %bitcast.125, s32[1024]{0:T(1024)S(1)} %bitcast.126, s32[1024]{0:T(1024)S(1)} %bitcast.127, s32[1024]{0:T(1024)S(1)} %bitcast.128, ...), kind=kOutput, calls=%fused_computation.84.clone.1 | convolution fusion | flops 71303168 | bytes 401408 | tf_op jit(solution)/shard_map/while/body/eval_jaxpr/dot_general | solution.py:82
  226.3 4.0 %fusion.176 = f32[512,16]{0,1:T(8,128)} fusion(s32[1024]{0:T(1024)S(1)} %bitcast.119, s32[1024]{0:T(1024)S(1)} %bitcast.120, s32[1024]{0:T(1024)S(1)} %bitcast.138, s32[1024]{0:T(1024)S(1)} %bitcast.139, s32[1024]{0:T(1024)S(1)} %bitcast.140, s32[1024]{0:T(1024)S(1)} %bitcast.141, s32[1024]{0:T(1024)S(1)} %bitcast.137, s32[1024]{0:T(1024)S(1)} %bitcast.118, ...), kind=kOutput, calls=%fused_computation.114.clone.1 | convolution fusion | flops 37748736 | bytes 335872 | tf_op jit(solution)/shard_map/while/body/eval_jaxpr/dot_general | solution.py:82
  232.4 2.0 copy.19
  (58 shorter events, 33.6 us)
Async XLA Ops:
  7.2 1.9 copy-start
  25.0 126.2 %all-to-all-start = ((bf16[128,32,384]{2,0,1:T(8,128)(2,1)}), bf16[128,32,384]{2,0,1:T(8,128)(2,1)}, u32[]{:S(2)}, u32[]{:S(2)}) async-start(bf16[128,32,384]{2,0,1:T(8,128)(2,1)} %fusion.134), calls=%async_computation | async-start | bytes 6291456 | tf_op jit(solution)/shard_map/all_to_all | solution.py:17
  31.4 203.1 %reduce-scatter.2.cloned.1.call-start = ((), (), s32[]{:S(2)}) async-start(), calls=%async_computation.2 | async-start | bytes 4325376 | tf_op jit(solution)/shard_map/reduce_scatter | solution.py:41
  43.7 2.5 %copy-start.1 = (bf16[128,32,384]{2,0,1:T(8,128)(2,1)S(1)}, bf16[128,32,384]{2,0,1:T(8,128)(2,1)}, u32[]{:S(2)}) copy-start(bf16[128,32,384]{2,0,1:T(8,128)(2,1)} %fusion.134) | copy-start | bytes 9437188
  49.8 1.0 copy-start.2
Sparse Core Ops, SparseCore 0:
  50.0 160.4 reduce-scatter.1
where the time goes:
time: 243 us; the launch traced here: 241 us
  waiting for transfers between devices  97.8 us (40%)
  matrix products  55.3 us (23%)
  local copies, waits for them, and re-layouts  45.2 us (19%)
  other arithmetic  22.1 us (9%)
  between operations  14.1 us (6%)
  starting transfers between devices  6.57 us (3%)
    all_to_all x1, waiting for transfers between devices, deliver(): lax.all_to_all(sending, ('node', 'local'), split_axis=1, concat_axis=0, t...  97.8 us
    dot_general x12, matrix products, accumulate(): lax.dot_general(hits, dpool_block[:, offset:offset + width], (((0,), (0,)...  48.8 us
    gather x2, local copies, waits for them, and re-layouts, local(): pool_send = jnp.take(pooled, assign, axis=1)  12.1 us
    gather x1, local copies, waits for them, and re-layouts, local(): grad_send = jnp.take(grad_out, assign, axis=1)  11.2 us
    add x4, other arithmetic, accumulate(): return (carry + jnp.concatenate(pieces, axis=1), None)  7.92 us
    dynamic_slice x16, local copies, waits for them, and re-layouts, local(): lax.scan(accumulate, start_total, (dpool_blocks, lookup_blocks, count_blo...  7.77 us
    all_to_all x1, starting transfers between devices, deliver(): lax.all_to_all(sending, ('node', 'local'), split_axis=1, concat_axis=0, t...  6.35 us
    unnamed x7, local copies, waits for them, and re-layouts  5.87 us
  transfers between devices with their start and end apart: 2, of which 1 were waited for; matrix products, arithmetic and copies ran while one was open for 43% of the time, Pallas kernels for 0%

commit v1 on v0

v1 whole, which is shorter than its diff:
```python
import functools
import math

import jax
import jax.numpy as jnp
from jax import lax
from jax.experimental import pallas as pl
from jax.experimental.pallas import tpu as pltpu
from jax.sharding import PartitionSpec as P

ROWS = 512
W1 = 16
W2 = 48
W3 = 192
PD = 128
W12 = W1 + W2
WSUM = W12 + W3
AXES = ("node", "local")
EB = 16
VMEM = 60 * 1024 * 1024


def params(*semantics):
    return pltpu.CompilerParams(dimension_semantics=semantics, vmem_limit_bytes=VMEM)


def cost(flops, nbytes):
    return pl.CostEstimate(flops=flops, bytes_accessed=nbytes, transcendentals=0)


def fill_permutation(assign_ref, perm_ref, slots):
    width = EB * slots
    lane = lax.broadcasted_iota(jnp.int32, (EB, width), 1)
    first = lax.broadcasted_iota(jnp.int32, (EB, width), 0) * slots

    def one(s, carry):
        start = pl.multiple_of(s * EB, EB)
        perm_ref[pl.ds(start, EB), :] = jnp.where(lane == first + assign_ref[s], 1.0, 0.0).astype(jnp.bfloat16)
        return carry

    lax.fori_loop(0, slots, one, 0)


def permute_one_kernel(slots, assign_ref, x_ref, out_ref, perm_ref):
    @pl.when(pl.program_id(0) == 0)
    def _():
        fill_permutation(assign_ref, perm_ref, slots)

    block = x_ref[...].reshape(EB * slots, x_ref.shape[2])
    moved = jnp.dot(perm_ref[...], block, preferred_element_type=jnp.float32)
    out_ref[...] = moved.astype(jnp.bfloat16).reshape(slots, EB, x_ref.shape[2])


def permute_one(assign, x, width, column):
    count, slots, _ = x.shape
    return pl.pallas_call(
        functools.partial(permute_one_kernel, slots),
        out_shape=jax.ShapeDtypeStruct((slots, count, width), x.dtype),
        grid_spec=pltpu.PrefetchScalarGridSpec(
            num_scalar_prefetch=1,
            grid=(count // EB,),
            in_specs=[pl.BlockSpec((EB, slots, width), lambda i, a: (i, 0, column))],
            out_specs=pl.BlockSpec((slots, EB, width), lambda i, a: (0, i, 0)),
            scratch_shapes=[pltpu.VMEM((EB * slots, EB * slots), jnp.bfloat16)],
        ),
        compiler_params=params("arbitrary"),
        cost_estimate=cost(2 * count * slots * EB * slots * width, 4 * count * slots * width),
        name="permute_sent",
    )(assign, x)


def permute_two_kernel(slots, assign_ref, x_ref, y_ref, xo_ref, yo_ref, perm_ref):
    @pl.when(pl.program_id(0) == 0)
    def _():
        fill_permutation(assign_ref, perm_ref, slots)

    for ref, out in ((x_ref, xo_ref), (y_ref, yo_ref)):
        block = ref[...].reshape(EB * slots, ref.shape[2])
        moved = jnp.dot(perm_ref[...], block, preferred_element_type=jnp.float32)
        out[...] = moved.astype(jnp.bfloat16).reshape(slots, EB, ref.shape[2])


def permute_two(assign, x, xw, y, yw):
    count, slots, _ = x.shape
    return pl.pallas_call(
        functools.partial(permute_two_kernel, slots),
        out_shape=(
            jax.ShapeDtypeStruct((slots, count, xw), x.dtype),
            jax.ShapeDtypeStruct((slots, count, yw), y.dtype),
        ),
        grid_spec=pltpu.PrefetchScalarGridSpec(
            num_scalar_prefetch=1,
            grid=(count // EB,),
            in_specs=[
                pl.BlockSpec((EB, slots, xw), lambda i, a: (i, 0, 0)),
                pl.BlockSpec((EB, slots, yw), lambda i, a: (i, 0, 0)),
            ],
            out_specs=[
                pl.BlockSpec((slots, EB, xw), lambda i, a: (0, i, 0)),
                pl.BlockSpec((slots, EB, yw), lambda i, a: (0, i, 0)),
            ],
            scratch_shapes=[pltpu.VMEM((EB * slots, EB * slots), jnp.bfloat16)],
        ),
        compiler_params=params("arbitrary"),
        cost_estimate=cost(2 * count * slots * EB * slots * (xw + yw), 4 * count * slots * (xw + yw)),
        name="permute_rest",
    )(assign, x, y)


def narrow_kernel(slots_step, g_ref, w_ref, out_ref):
    half = g_ref.shape[1] // 2
    row = lax.broadcasted_iota(jnp.int32, (W12, PD), 0)
    for s in range(slots_step):
        w = w_ref[s].astype(jnp.float32)
        first = jnp.where(row < W1, w, 0.0).astype(jnp.bfloat16)
        second = jnp.where(row < W1, 0.0, w).astype(jnp.bfloat16)
        weights = jnp.concatenate([first, second], axis=1)
        d = lax.dot_general(g_ref[s], weights, (((1,), (1,)), ((), ())), preferred_element_type=jnp.float32)
        out_ref[s] = jnp.concatenate([d[:half], d[half:]], axis=1).astype(jnp.bfloat16)


def narrow_dpool(g12, w12):
    slots, count, _ = g12.shape
    step = 4
    return pl.pallas_call(
        functools.partial(narrow_kernel, step),
        out_shape=jax.ShapeDtypeStruct((slots, count // 2, 2 * W12), jnp.bfloat16),
        grid=(slots // step,),
        in_specs=[
            pl.BlockSpec((step, count, 2 * PD), lambda i: (i, 0, 0)),
            pl.BlockSpec((step, W12, PD), lambda i: (i, 0, 0)),
        ],
        out_specs=pl.BlockSpec((step, count // 2, 2 * W12), lambda i: (i, 0, 0)),
        compiler_params=params("arbitrary"),
        cost_estimate=cost(4 * slots * count * W12 * PD, slots * count * 6 * PD),
        name="narrow_dpool",
    )(g12, w12)


def partial_kernel(order_ref, q_ref, g12_ref, g3_ref, out_ref):
    step = out_ref.shape[0]
    for p in range(step):
        slot = order_ref[pl.program_id(0) * step + p]
        q = q_ref[slot]
        g = jnp.concatenate([g12_ref[slot], g3_ref[slot]], axis=1)
        dims = (((0,), (0,)), ((), ()))
        full = lax.dot_general(q, g, dims, preferred_element_type=jnp.float32)
        out_ref[p, :W1] = full[:W1, :PD]
        out_ref[p, W1:W12] = full[W1:W12, PD : 2 * PD]
        out_ref[p, W12:] = full[W12:, 2 * PD :]


def partial_proj(order, q, g12, g3):
    slots, count, _ = q.shape
    chosen = order.shape[0]
    step = 4
    return pl.pallas_call(
        partial_kernel,
        out_shape=jax.ShapeDtypeStruct((chosen, WSUM, PD), jnp.float32),
        grid_spec=pltpu.PrefetchScalarGridSpec(
            num_scalar_prefetch=1,
            grid=(chosen // step,),
            in_specs=[
                pl.BlockSpec((slots, count, WSUM), lambda i, o: (0, 0, 0)),
                pl.BlockSpec((slots, count, 2 * PD), lambda i, o: (0, 0, 0)),
                pl.BlockSpec((slots, count, PD), lambda i, o: (0, 0, 0)),
            ],
            out_specs=pl.BlockSpec((step, WSUM, PD), lambda i, o: (i, 0, 0)),
        ),
        compiler_params=params("arbitrary"),
        cost_estimate=cost(2 * chosen * count * WSUM * 3 * PD, slots * count * 1280 + chosen * WSUM * PD * 4),
        name="partial_proj",
    )(order, q, g12, g3)


def hits_kernel(index_ref, length_ref, out_ref):
    lookups, block = index_ref.shape[1], index_ref.shape[2]
    rows = out_ref.shape[1]
    half = rows // 2
    chunk = 16
    index = index_ref[0]
    which = lax.broadcasted_iota(jnp.int32, (lookups, block), 0)
    index = jnp.where(which < length_ref[0], index, -1)
    ids = lax.broadcasted_iota(jnp.int32, (chunk, block), 0).astype(jnp.float32).astype(jnp.bfloat16)
    for part in range(2):
        wanted = (index - part * half).astype(jnp.float32)
        wide = [
            jnp.broadcast_to(wanted[j : j + 1], (chunk, block)).astype(jnp.bfloat16) for j in range(lookups)
        ]
        for r in range(half // chunk):
            row = ids + jnp.bfloat16(r * chunk)
            total = jnp.zeros((chunk, block), jnp.bfloat16)
            for j in range(lookups):
                total = total + jnp.where(wide[j] == row, jnp.bfloat16(1), jnp.bfloat16(0))
            start = part * half + r * chunk
            out_ref[0, start : start + chunk, :] = total


def count_hits(lookups, counts):
    tables, bag, examples = lookups.shape
    block = 512
    return pl.pallas_call(
        hits_kernel,
        out_shape=jax.ShapeDtypeStruct((tables, ROWS, examples), jnp.bfloat16),
        grid=(tables, examples // block),
        in_specs=[
            pl.BlockSpec((1, bag, block), lambda k, i: (k, 0, i)),
            pl.BlockSpec((1, 1, block), lambda k, i: (k, 0, i)),
        ],
        out_specs=pl.BlockSpec((1, ROWS, block), lambda k, i: (k, 0, i)),
        compiler_params=params("arbitrary", "arbitrary"),
        cost_estimate=cost(tables * ROWS * examples * bag * 3, tables * examples * (ROWS * 2 + 36)),
        name="count_hits",
    )(lookups, counts)


def table_kernel(hits_ref, g3_ref, narrow_ref, w_ref, out_ref):
    block = g3_ref.shape[0]
    sources, half, _ = narrow_ref.shape

    @pl.when(pl.program_id(0) == 0)
    def _():
        out_ref[...] = jnp.zeros_like(out_ref)

    column = lax.broadcasted_iota(jnp.int32, (block, WSUM), 1)
    d3 = lax.dot_general(g3_ref[...], w_ref[...], (((1,), (1,)), ((), ())), preferred_element_type=jnp.float32)
    d3 = jnp.where(column < W12, 0.0, d3).astype(jnp.bfloat16)
    pieces = []
    for d in range(sources):
        packed = narrow_ref[d].astype(jnp.float32)
        pieces += [packed[:, :W12], packed[:, W12:]]
    d12 = jnp.concatenate(pieces, axis=0)
    d12 = jnp.concatenate([d12, jnp.zeros((block, WSUM - W12), jnp.float32)], axis=1)
    d1 = jnp.where(column < W1, d12, 0.0).astype(jnp.bfloat16)
    d2 = jnp.where(column < W1, 0.0, d12).astype(jnp.bfloat16)
    out_ref[...] += (
        jnp.dot(hits_ref[0], d1, preferred_element_type=jnp.float32)
        + jnp.dot(hits_ref[1], d2, preferred_element_type=jnp.float32)
        + jnp.dot(hits_ref[2], d3, preferred_element_type=jnp.float32)
    )


def table_sum(hits, g3, narrow, weights):
    tables, rows, examples = hits.shape
    sources, half, _ = narrow.shape
    block = 512
    per = block // (2 * half)
    return pl.pallas_call(
        table_kernel,
        out_shape=jax.ShapeDtypeStruct((rows, WSUM), jnp.float32),
        grid=(examples // block,),
        in_specs=[
            pl.BlockSpec((tables, rows, block), lambda i: (0, 0, i)),
            pl.BlockSpec((block, PD), lambda i: (i, 0)),
            pl.BlockSpec((per, half, 2 * W12), lambda i: (i, 0, 0)),
            pl.BlockSpec((WSUM, PD), lambda i: (0, 0)),
        ],
        out_specs=pl.BlockSpec((rows, WSUM), lambda i: (0, 0)),
        compiler_params=params("arbitrary"),
        cost_estimate=cost(6 * rows * examples * WSUM, hits.size * 2 + examples * 400 + rows * WSUM * 4),
        name="table_sum",
    )(hits, g3, narrow, weights)


def bits_of(size):
    return [1 << b for b in range(size.bit_length() - 1)]


def swap(x, axis, size, bit):
    return lax.ppermute(x, axis, [(d, d ^ bit) for d in range(size)])


def halve(kept, sent, path, sizes):
    for n, (axis, bit) in enumerate(path):
        got = swap(sent, axis, sizes[axis], bit)
        half = kept.shape[0] // 2
        if n + 1 < len(path):
            sent = kept[half:] + got[half:]
            kept = kept[:half] + got[:half]
        else:
            kept = kept + got
    return kept


def local(sizes, grad_out, pooled, proj, assign, indices, lengths):
    count, slots, _ = grad_out.shape
    scale = 1.0 / math.sqrt(count * slots)
    n_node, n_local = sizes["node"], sizes["local"]

    w12 = lax.all_gather(proj[0, :W12], AXES, axis=0, tiled=False)
    g3 = permute_one(assign, grad_out, PD, 2)
    g3_got = lax.all_to_all(g3, AXES, split_axis=0, concat_axis=0, tiled=True).reshape(-1, PD)
    g12, q = permute_two(assign, grad_out, 2 * PD, pooled, WSUM)
    narrow = narrow_dpool(g12, w12)
    narrow_got = lax.all_to_all(narrow, AXES, split_axis=0, concat_axis=0, tiled=True)

    node, loc = lax.axis_index("node"), lax.axis_index("local")
    core = [("node", 1)]
    nodes = [("node", b) for b in bits_of(n_node)[1:]]
    locals_ = [("local", b) for b in bits_of(n_local)]
    path_a = core + nodes + locals_

    def slot_order(path):
        position = jnp.arange(slots, dtype=jnp.int32)
        flip = jnp.zeros((slots,), jnp.int32)
        for n, (axis, bit) in enumerate(path):
            on = (position >> (len(path) - 1 - n)) & 1
            flip = flip + on * bit * (n_local if axis == "node" else 1)
        return flip ^ (node * n_local + loc).astype(jnp.int32)

    order = slot_order(path_a)
    sent = partial_proj(order[slots // 2 :], q, g12, g3)
    kept = partial_proj(order[: slots // 2], q, g12, g3)
    got = swap(sent, "node", n_node, 1)
    rows = WSUM // 2
    shape = [2] * len(nodes) + [n_local, rows, PD]
    back = list(range(len(nodes)))[::-1] + [len(nodes), len(nodes) + 1, len(nodes) + 2]
    halves = []
    for part in range(2):
        cut = slice(part * rows, (part + 1) * rows)

        def laid(x):
            x = x[:, cut]
            if part:
                x = x.reshape(shape).transpose(back).reshape(x.shape)
            return x

        total = laid(kept) + laid(got)
        path = (nodes if part == 0 else nodes[::-1]) + locals_
        half = total.shape[0] // 2
        halves.append(halve(total[:half], total[half:], path, sizes))
    proj_grad = jnp.concatenate(halves, axis=1) * scale

    lookups = indices[0].transpose(1, 2, 0)
    counts = lengths[0].T[:, None, :]
    hits = count_hits(lookups, counts)
    table_grad = table_sum(hits, g3_got, narrow_got, proj[0])[None]
    return (table_grad, proj_grad)


def solution(mesh):
    placed = (
        P(AXES, None, None),
        P(AXES, None, None),
        P(AXES, None, None),
        P(),
        P(AXES, None, None, None),
        P(AXES, None, None),
    )
    return jax.shard_map(
        functools.partial(local, dict(mesh.shape)),
        mesh=mesh,
        in_specs=placed,
        out_specs=(P(AXES, None, None), P(AXES, None, None)),
        check_vma=False,
    )
```

time: 243 us -> 194 us (0.80)
  the two profiles are of different devices: /device:TPU:13 before, /device:TPU:0 now
where the time goes in v1:
time: 194 us; the launch traced here: 192 us
  blocking collectives  96.7 us (50%)
  Pallas kernels  62.9 us (32%)
  starting transfers between devices  15.5 us (8%)
  waiting for transfers between devices  7.3 us (4%)
  other arithmetic  4.35 us (2%)
  local copies, waits for them, and re-layouts  4.06 us (2%)
    all_gather x1, blocking collectives, local(): w12 = lax.all_gather(proj[0, :W12], AXES, axis=0, tiled=False)  79 us
    all_to_all x1, blocking collectives, local(): lax.all_to_all(narrow, AXES, split_axis=0, concat_axis=0, tiled=True)  17.7 us
    pallas_call x1, Pallas kernels, count_hits(): pl.pallas_call(hits_kernel, out_shape=jax.ShapeDtypeStruct((tables, ROWS,...  17.6 us
    pallas_call x2, Pallas kernels, partial_proj(): pl.pallas_call(partial_kernel, out_shape=jax.ShapeDtypeStruct((chosen, WS...  12.2 us
    ppermute x9, starting transfers between devices, swap(): return lax.ppermute(x, axis, [(d, d ^ bit) for d in range(size)])  11.4 us
    pallas_call x1, Pallas kernels, table_sum(): pl.pallas_call(table_kernel, out_shape=jax.ShapeDtypeStruct((rows, WSUM),...  10.6 us
    pallas_call x1, Pallas kernels, permute_two(): pl.pallas_call(functools.partial(permute_two_kernel, slots), out_shape=(j...  9.05 us
    ppermute x9, waiting for transfers between devices, swap(): return lax.ppermute(x, axis, [(d, d ^ bit) for d in range(size)])  7.3 us
  transfers between devices with their start and end apart: 10, of which 3 were waited for; matrix products, arithmetic and copies ran while one was open for 3% of the time, Pallas kernels for 21%

profile of v1, /device:TPU:0, one launch (start us, length us, event | category | flops | bytes accessed | tf_op | source)
XLA Modules:
  0.0 191.6 jit_solution(10776924166317658489)
XLA Ops:
  1.2 7.2 %permute_sent.1.g3_ref = bf16[32,128,128]{2,1,0:T(8,128)(2,1)} custom-call(s32[32]{0:T(128)} %assign_ref.3, bf16[128,32,384]{2,1,0:T(8,128)(2,1)} %x_ref.3), custom_call_target="tpu_custom_call" | custom-call | flops 536870912 | bytes 2097152 | tf_op jit(solution)/shard_map/permute_sent/pallas_call | solution.py:56
  8.4 9.1 %permute_rest.1 = (bf16[32,128,256]{2,1,0:T(8,128)(2,1)}, bf16[32,128,256]{2,1,0:T(8,128)(2,1)}) custom-call(s32[32]{0:T(128)} %assign_ref.3, bf16[128,32,384]{2,1,0:T(8,128)(2,1)} %x_ref.3, bf16[128,32,256]{2,1,0:T(8,128)(2,1)} %y_ref.1), custom_call_target="tpu_custom_call" | custom-call | flops 2147483648 | bytes 8388608 | tf_op jit(solution)/shard_map/permute_rest/pallas_call | solution.py:85
  17.5 6.1 %partial_proj.3 = f32[16,256,128]{2,1,0:T(8,128)} custom-call(s32[16]{0:T(128)} %get-tuple-element.17.order_ref, bf16[32,128,256]{2,1,0:T(8,128)(2,1)} %get-tuple-element.5.q_ref, bf16[32,128,256]{2,1,0:T(8,128)(2,1)} %get-tuple-element.4.g_ref.g12_ref, bf16[32,128,128]{2,1,0:T(8,128)(2,1)} %permute_sent.1.g3_ref), custom_call_target="tpu_custom_call" | custom-call | flops 402653184 | bytes 7340032 | tf_op jit(solution)/shard_map/partial_proj/pallas_call | solution.py:157
  24.1 79.0 %all_gather.3.w_ref = bf16[32,64,128]{2,1,0:T(8,128)(2,1)} all-gather(bf16[1,64,128]{2,1,0:T(8,128)(2,1)S(1)} %slice-done), channel_id=1, replica_groups=mesh['node'=8,'local'=4] {'node','local'}, dimensions={0}, use_global_device_ids=true | all-gather | bytes 540672 | tf_op jit(solution)/shard_map/all_gather | solution.py:290
  103.1 6.3 %narrow_dpool.1 = bf16[32,64,128]{2,1,0:T(8,128)(2,1)} custom-call(bf16[32,128,256]{2,1,0:T(8,128)(2,1)} %get-tuple-element.4.g_ref.g12_ref, bf16[32,64,128]{2,1,0:T(8,128)(2,1)} %all_gather.3.w_ref), custom_call_target="tpu_custom_call" | custom-call | flops 134217728 | bytes 3145728 | tf_op jit(solution)/shard_map/narrow_dpool/pallas_call | solution.py:125
  109.4 17.7 %all_to_all.10.narrow_ref = bf16[32,64,128]{2,1,0:T(8,128)(2,1)} all-to-all(bf16[32,64,128]{2,1,0:T(8,128)(2,1)} %narrow_dpool.1), channel_id=1, replica_groups=mesh['node'=8,'local'=4] {'node','local'}, dimensions={0} | all-to-all | bytes 1048576 | tf_op jit(solution)/shard_map/all_to_all | solution.py:295
  127.1 4.0 %all-to-all-start = ((bf16[32,128,128]{2,1,0:T(8,128)(2,1)}), bf16[32,128,128]{2,1,0:T(8,128)(2,1)S(1)}, u32[]{:S(2)}, u32[]{:S(2)}) async-start(bf16[32,128,128]{2,1,0:T(8,128)(2,1)} %permute_sent.1.g3_ref), calls=%async_computation | async-start | bytes 2097152 | tf_op jit(solution)/shard_map/all_to_all | solution.py:292
  131.2 6.1 %partial_proj.2 = f32[16,256,128]{2,1,0:T(8,128)} custom-call(s32[16]{0:T(128)} %get-tuple-element.16.order_ref, bf16[32,128,256]{2,1,0:T(8,128)(2,1)} %get-tuple-element.5.q_ref, bf16[32,128,256]{2,1,0:T(8,128)(2,1)} %get-tuple-element.4.g_ref.g12_ref, bf16[32,128,128]{2,1,0:T(8,128)(2,1)} %permute_sent.1.g3_ref), custom_call_target="tpu_custom_call" | custom-call | flops 402653184 | bytes 7340032 | tf_op jit(solution)/shard_map/partial_proj/pallas_call | solution.py:157
  137.2 2.4 %slice_add_fusion.1 = (f32[16,128,128]{2,1,0:T(8,128)S(1)}, f32[16,128,128]{2,1,0:T(8,128)S(1)}) fusion(f32[16,256,128]{2,1,0:T(8,128)} %collective-permute-done, f32[16,256,128]{2,1,0:T(8,128)} %partial_proj.2), kind=kLoop, calls=%fused_computation.1 | loop fusion | flops 524288 | bytes 6291456 | tf_op jit(solution)/shard_map/add | solution.py:328
  139.7 0.8 slice.145
  140.5 1.8 collective-permute-start.1
  142.3 0.8 slice.160
  143.1 1.5 collective-permute-start.5
  145.3 17.6 %count_hits.1.hits_ref = bf16[3,512,4096]{2,1,0:T(8,128)(2,1)} custom-call(s32[3,8,4096]{2,1,0:T(8,128)} %bitcast.21, s32[3,1,4096]{2,1,0:T(1,128)} %broadcast_in_dim.6.length_ref), custom_call_target="tpu_custom_call" | custom-call | flops 150994944 | bytes 13025280 | tf_op jit(solution)/shard_map/count_hits/pallas_call | solution.py:202
  163.0 1.1 slice_add_fusion.5
  165.1 1.0 copy-done
  166.1 10.6 %table_sum.1 = f32[512,256]{1,0:T(8,128)} custom-call(bf16[3,512,4096]{2,1,0:T(8,128)(2,1)} %count_hits.1.hits_ref, bf16[4096,128]{1,0:T(8,128)(2,1)} %bitcast.18, bf16[32,64,128]{2,1,0:T(8,128)(2,1)} %all_to_all.10.narrow_ref, bf16[256,128]{1,0:T(8,128)(2,1)} %bitcast.23), custom_call_target="tpu_custom_call" | custom-call | flops 3221225472 | bytes 14745600 | tf_op jit(solution)/shard_map/table_sum/pallas_call | solution.py:248
  176.7 1.8 collective-permute-start.3
  178.9 3.9 %collective-permute-done.3 = f32[2,128,128]{2,1,0:T(8,128)S(1)} collective-permute-done((f32[2,128,128]{2,1,0:T(8,128)S(1)}, f32[2,128,128]{2,1,0:T(8,128)S(1)}, u32[]{:S(2)}, u32[]{:S(2)}) %collective-permute-start.3) | collective-permute-done | bytes 131104 | tf_op jit(solution)/shard_map/ppermute | solution.py:270
  182.8 2.8 %collective-permute-start.4 = (f32[1,128,128]{2,1,0:T(8,128)S(1)}, f32[1,128,128]{2,1,0:T(8,128)S(1)}, u32[]{:S(2)}, u32[]{:S(2)}) collective-permute-start(f32[1,128,128]{2,1,0:T(8,128)S(1)} %slice_add_fusion.12), channel_id=1, source_target_pairs={{0,2},{1,3},{2,0},{3,1},{4,6},{5,7},{6,4},{7,5},{8,10},{9,11},{10,... | collective-permute-start | bytes 196616 | tf_op jit(solution)/shard_map/ppermute | solution.py:270
  185.6 1.8 collective-permute-start.8
  187.5 0.9 collective-permute-done.4
  188.4 2.5 %collective-permute-done.8 = f32[1,128,128]{2,1,0:T(8,128)S(1)} collective-permute-done((f32[1,128,128]{2,1,0:T(8,128)S(1)}, f32[1,128,128]{2,1,0:T(8,128)S(1)}, u32[]{:S(2)}, u32[]{:S(2)}) %collective-permute-start.8) | collective-permute-done | bytes 65568 | tf_op jit(solution)/shard_map/ppermute | solution.py:270
  190.9 0.7 maximum_multiply_fusion
  (28 shorter events, 3.3 us)
Async XLA Ops:
  17.5 6.6 %slice-start = ((bf16[1,256,128]{2,1,0:T(8,128)(2,1)}), bf16[1,64,128]{2,1,0:T(8,128)(2,1)S(1)}, s32[]{:S(2)}) async-start(bf16[1,256,128]{2,1,0:T(8,128)(2,1)} %param.8), calls=%async_computation.2 | async-start | bytes 32768 | tf_op jit(solution)/shard_map/slice | solution.py:290
  23.6 113.6 %collective-permute-start = (f32[16,256,128]{2,1,0:T(8,128)}, f32[16,256,128]{2,1,0:T(8,128)}, u32[]{:S(2)}, u32[]{:S(2)}) collective-permute-start(f32[16,256,128]{2,1,0:T(8,128)} %partial_proj.3), channel_id=1, source_target_pairs={{0,4},{4,0},{8,12},{12,8},{16,20},{20,16},{24,28},{28,24},{1,5},{5... | collective-permute-start | bytes 6291464 | tf_op jit(solution)/shard_map/ppermute | solution.py:270
  127.1 38.0 %all-to-all-start = ((bf16[32,128,128]{2,1,0:T(8,128)(2,1)}), bf16[32,128,128]{2,1,0:T(8,128)(2,1)S(1)}, u32[]{:S(2)}, u32[]{:S(2)}) async-start(bf16[32,128,128]{2,1,0:T(8,128)(2,1)} %permute_sent.1.g3_ref), calls=%async_computation | async-start | bytes 2097152 | tf_op jit(solution)/shard_map/all_to_all | solution.py:292
  139.7 4.9 %copy-start.1 = (s32[1,4096,3]{1,0,2:T(1,128)S(1)}, s32[1,4096,3]{1,0,2:T(1,128)}, u32[]{:S(2)}) copy-start(s32[1,4096,3]{1,0,2:T(1,128)} %param.11) | copy-start | bytes 147460
  140.5 22.4 %collective-permute-start.1 = (f32[8,128,128]{2,1,0:T(8,128)}, f32[8,128,128]{2,1,0:T(8,128)}, u32[]{:S(2)}, u32[]{:S(2)}) collective-permute-start(f32[8,128,128]{2,1,0:T(8,128)} %slice.145), channel_id=1, source_target_pairs={{0,8},{4,12},{8,0},{12,4},{16,24},{20,28},{24,16},{28,20},{1,9},{5... | collective-permute-start | bytes 1572872 | tf_op jit(solution)/shard_map/ppermute | solution.py:270
  143.1 21.6 %collective-permute-start.5 = (f32[8,128,128]{2,1,0:T(8,128)}, f32[8,128,128]{2,1,0:T(8,128)S(1)}, u32[]{:S(2)}, u32[]{:S(2)}) collective-permute-start(f32[8,128,128]{2,1,0:T(8,128)} %bitcast.10), channel_id=1, source_target_pairs={{0,16},{4,20},{8,24},{12,28},{16,0},{20,4},{24,8},{28,12},{1,17},{... | collective-permute-start | bytes 1572872 | tf_op jit(solution)/shard_map/ppermute | solution.py:270
  164.1 12.6 %collective-permute-start.2 = (f32[4,128,128]{2,1,0:T(8,128)S(1)}, f32[4,128,128]{2,1,0:T(8,128)S(1)}, u32[]{:S(2)}, u32[]{:S(2)}) collective-permute-start(f32[4,128,128]{2,1,0:T(8,128)S(1)} %get-tuple-element.9), channel_id=1, source_target_pairs={{0,16},{4,20},{8,24},{12,28},{16,0},{20,4},{24,8},{28,12},{1,17},{... | collective-permute-start | bytes 786440 | tf_op jit(solution)/shard_map/ppermute | solution.py:270
  164.7 13.8 %collective-permute-start.6 = (f32[4,128,128]{2,1,0:T(8,128)S(1)}, f32[4,128,128]{2,1,0:T(8,128)S(1)}, u32[]{:S(2)}, u32[]{:S(2)}) collective-permute-start(f32[4,128,128]{2,1,0:T(8,128)S(1)} %get-tuple-element.11), channel_id=1, source_target_pairs={{0,8},{4,12},{8,0},{12,4},{16,24},{20,28},{24,16},{28,20},{1,9},{5... | collective-permute-start | bytes 786440 | tf_op jit(solution)/shard_map/ppermute | solution.py:270
  165.1 1.0 copy-start
  176.7 6.1 %collective-permute-start.3 = (f32[2,128,128]{2,1,0:T(8,128)S(1)}, f32[2,128,128]{2,1,0:T(8,128)S(1)}, u32[]{:S(2)}, u32[]{:S(2)}) collective-permute-start(f32[2,128,128]{2,1,0:T(8,128)S(1)} %get-tuple-element.13), channel_id=1, source_target_pairs={{0,1},{1,0},{2,3},{3,2},{4,5},{5,4},{6,7},{7,6},{8,9},{9,8},{10,11... | collective-permute-start | bytes 393224 | tf_op jit(solution)/shard_map/ppermute | solution.py:270
  178.6 7.0 %collective-permute-start.7 = (f32[2,128,128]{2,1,0:T(8,128)S(1)}, f32[2,128,128]{2,1,0:T(8,128)S(1)}, u32[]{:S(2)}, u32[]{:S(2)}) collective-permute-start(f32[2,128,128]{2,1,0:T(8,128)S(1)} %get-tuple-element.15), channel_id=1, source_target_pairs={{0,1},{1,0},{2,3},{3,2},{4,5},{5,4},{6,7},{7,6},{8,9},{9,8},{10,11... | collective-permute-start | bytes 393224 | tf_op jit(solution)/shard_map/ppermute | solution.py:270
  182.8 5.5 %collective-permute-start.4 = (f32[1,128,128]{2,1,0:T(8,128)S(1)}, f32[1,128,128]{2,1,0:T(8,128)S(1)}, u32[]{:S(2)}, u32[]{:S(2)}) collective-permute-start(f32[1,128,128]{2,1,0:T(8,128)S(1)} %slice_add_fusion.12), channel_id=1, source_target_pairs={{0,2},{1,3},{2,0},{3,1},{4,6},{5,7},{6,4},{7,5},{8,10},{9,11},{10,... | collective-permute-start | bytes 196616 | tf_op jit(solution)/shard_map/ppermute | solution.py:270
  185.6 5.2 %collective-permute-start.8 = (f32[1,128,128]{2,1,0:T(8,128)S(1)}, f32[1,128,128]{2,1,0:T(8,128)S(1)}, u32[]{:S(2)}, u32[]{:S(2)}) collective-permute-start(f32[1,128,128]{2,1,0:T(8,128)S(1)} %slice_add_fusion.10), channel_id=1, source_target_pairs={{0,2},{1,3},{2,0},{3,1},{4,6},{5,7},{6,4},{7,5},{8,10},{9,11},{10,... | collective-permute-start | bytes 196616 | tf_op jit(solution)/shard_map/ppermute | solution.py:270
